TPU v7x, 32 devices: a whole 2x2x4 slice. The times are simulated.
32 devices in a mesh: dp: 8 (over z, x), outer: 4 (over y, core).
Axes of the slice: x: 2, y: 2, z: 4, core: 2. Of those that a mesh axis runs over, the one named last changes fastest.
Arguments:
- image_embeds: bfloat16 [4, 2048, 1152], P('outer', 'dp'), may hold values from -6 to 6
- text_features: bfloat16 [4, 2048, 1152], P('outer', 'dp'), may hold values from -92 to 92
- projection: bfloat16 [1152, 1152], replicated, may hold values from -0.1875 to 0.1875
- pair_step: int32 [4, 2048], P('outer'), may hold values from 0 to 5
- pair_col: int32 [4, 2048], P('outer'), may hold values from 0 to 255
Outputs:
- grad_text: bfloat16 [4, 2048, 1152], P('outer', 'dp')
- grad_proj: float32 [1152, 1152], P('dp', 'outer')
Inputs may be any that keep to these rules, and one draw needn't show every extreme that they name: pair_step of image row i in shard a points at text shard a - pair_step + 2 of the same group.
All inputs are finite; a program needn't handle non-finite values.
Results may differ from a plain program's by a relative error of at most 0.02.
Values may be sent and summed in bfloat16 or wider, within the bound.
A program may use at most 64 MiB of HBM per device.

v0:
```python
import math

import jax
import jax.numpy as jnp
from jax import lax
from jax.sharding import PartitionSpec as P

WINDOW = 6


LOGIT_SCALE = 10.0
LOGIT_BIAS = -3.0
LOSS_SCALE = 256.0
EPSILON = 1e-06


def shifted(value, axis, steps):
    count = lax.axis_size(axis)
    pairs = [(source, (source + steps) % count) for source in range(count)]
    return lax.ppermute(value, axis, pairs)


def unit_rows(values):
    values = values.astype(jnp.float32)
    inverse = lax.rsqrt(jnp.sum(values * values, axis=-1, keepdims=True) + EPSILON)
    return (values * inverse, inverse)


def pair_grad(images, texts, step_ids, col_ids, position):
    logits = (
        LOGIT_SCALE * jnp.einsum("ie,ke->ik", images, texts, preferred_element_type=jnp.float32)
        + LOGIT_BIAS
    )
    columns = lax.broadcasted_iota(jnp.int32, logits.shape, 1)
    positive = (step_ids[:, None] == position) & (col_ids[:, None] == columns)
    target = jnp.where(positive, 1.0, -1.0).astype(jnp.float32)
    return (-LOSS_SCALE * LOGIT_SCALE * target * jax.nn.sigmoid(-target * logits)).astype(
        jnp.bfloat16
    )


def shard_rows(table, shard, cycle_size, row_count):
    start = (shard + cycle_size) % cycle_size * row_count
    return lax.dynamic_slice_in_dim(table, start, row_count)


def move_block(travel, hop):
    return shifted(travel, "dp", hop)


def local(image_embeds, text_features, projection, pair_step, pair_col):
    cycle_size = lax.axis_size("dp")
    my_index = lax.axis_index("dp")
    row_count = image_embeds.shape[1]
    window_len = min(WINDOW, cycle_size)
    back_reach = window_len // 2 - 1
    unit_img = unit_rows(image_embeds[0])[0].astype(jnp.bfloat16)
    features = text_features[0]
    hidden = jnp.dot(features, projection, preferred_element_type=jnp.float32)
    unit_text, inverse_norm = unit_rows(hidden)
    text_units = unit_text.astype(jnp.bfloat16)
    all_steps = pair_step[0]
    all_cols = pair_col[0]
    streams = [(-back_reach, 0)] + [(1, position) for position in range(1, window_len)]
    my_steps = shard_rows(all_steps, my_index, cycle_size, row_count)
    my_cols = shard_rows(all_cols, my_index, cycle_size, row_count)
    travel = text_units
    running = None
    for hop, position in streams:
        travel = move_block(travel, hop)
        if running is not None:
            running = shifted(running.astype(jnp.bfloat16), "dp", hop).astype(running.dtype)
        weights = pair_grad(unit_img, travel, my_steps, my_cols, position)
        contribution = jnp.einsum(
            "ik,ie->ke", weights, unit_img, preferred_element_type=jnp.float32
        )
        running = contribution if running is None else running + contribution
    unit_grad = shifted(running.astype(jnp.bfloat16), "dp", back_reach - streams[-1][1]).astype(
        running.dtype
    )
    radial = jnp.sum(unit_text * unit_grad, axis=-1, keepdims=True)
    hidden_grad = (inverse_norm * (unit_grad - unit_text * radial)).astype(jnp.bfloat16)
    grad_text = jnp.einsum(
        "ke,de->kd", hidden_grad, projection, preferred_element_type=jnp.float32
    ).astype(jnp.bfloat16)
    partial_value = jnp.einsum(
        "kd,ke->de", features, hidden_grad, preferred_element_type=jnp.float32
    )
    partial_value = lax.optimization_barrier(partial_value.astype(jnp.bfloat16)).astype(jnp.float32)
    pooled = lax.psum_scatter(
        partial_value.astype(jnp.bfloat16), "outer", scatter_dimension=1, tiled=True
    ).astype(jnp.float32)
    owned = lax.psum_scatter(pooled, "dp", scatter_dimension=0, tiled=True)
    global_sq = lax.psum(jnp.sum(owned * owned), ("dp", "outer"))
    threshold = math.sqrt(projection.shape[0] * projection.shape[1])
    factor = jnp.minimum(1.0, threshold / jnp.sqrt(global_sq))
    return (grad_text[None], owned * factor)


def solution(mesh):
    placed = (
        P("outer", "dp", None),
        P("outer", "dp", None),
        P(),
        P("outer", None),
        P("outer", None),
    )
    return jax.shard_map(
        local,
        mesh=mesh,
        in_specs=placed,
        out_specs=(P("outer", "dp", None), P("dp", "outer")),
        check_vma=False,
    )
```

profile of v0, /device:TPU:0, one launch (start us, length us, event | category | flops | bytes accessed | tf_op | source)
XLA Modules:
  0.0 373.9 jit_solution(7413946674889123918)
XLA Ops:
  7.2 0.0 copy-start
  7.2 0.0 reduce-scatter.5.cloned.1.call-start
  7.2 1.7 copy-done
  8.9 2.1 multiply_reduce_fusion
  11.1 1.0 copy-done.1
  12.1 0.1 multiply_convert_fusion
  12.2 5.1 %collective-permute-start = (bf16[256,1152]{1,0:T(8,128)(2,1)S(1)}, bf16[256,1152]{1,0:T(8,128)(2,1)}, u32[]{:S(2)}, u32[]{:S(2)}) collective-permute-start(bf16[256,1152]{1,0:T(8,128)(2,1)S(1)} %multiply_convert_fusion), channel_id=1, source_target_pairs={{0,24},{4,28},{8,0},{12,4},{16,8},{20,12},{24,16},{28,20},{1,25},{... | collective-permute-start | bytes 1769480 | tf_op jit(solution)/shard_map/ppermute | solution.py:20
  17.3 0.7 compare_reduce_fusion
  18.0 0.7 constant_dynamic-slice_fusion
  18.7 1.3 fusion.5
  20.0 9.9 %collective-permute-done = bf16[256,1152]{1,0:T(8,128)(2,1)} collective-permute-done((bf16[256,1152]{1,0:T(8,128)(2,1)S(1)}, bf16[256,1152]{1,0:T(8,128)(2,1)}, u32[]{:S(2)}, u32[]{:S(2)}) %collective-permute-start) | collective-permute-done | bytes 589856 | tf_op jit(solution)/shard_map/ppermute | solution.py:20
  29.9 3.4 convolution_convert_fusion.2
  33.3 1.5 collective-permute-start.1
  34.8 0.5 collective-permute-start.2
  35.3 17.8 %collective-permute-done.1 = bf16[256,1152]{1,0:T(8,128)(2,1)} collective-permute-done((bf16[256,1152]{1,0:T(8,128)(2,1)}, bf16[256,1152]{1,0:T(8,128)(2,1)}, u32[]{:S(2)}, u32[]{:S(2)}) %collective-permute-start.1) | collective-permute-done | bytes 589856 | tf_op jit(solution)/shard_map/ppermute | solution.py:20
  53.1 10.9 %collective-permute-done.2 = bf16[256,1152]{1,0:T(8,128)(2,1)} collective-permute-done((bf16[256,1152]{1,0:T(8,128)(2,1)}, bf16[256,1152]{1,0:T(8,128)(2,1)}, u32[]{:S(2)}, u32[]{:S(2)}) %collective-permute-start.2) | collective-permute-done | bytes 589856 | tf_op jit(solution)/shard_map/ppermute | solution.py:20
  64.0 3.1 add_convert_fusion.4
  67.1 0.0 collective-permute-start.3
  67.1 0.0 collective-permute-start.4
  67.1 19.3 %collective-permute-done.3 = bf16[256,1152]{1,0:T(8,128)(2,1)} collective-permute-done((bf16[256,1152]{1,0:T(8,128)(2,1)}, bf16[256,1152]{1,0:T(8,128)(2,1)}, u32[]{:S(2)}, u32[]{:S(2)}) %collective-permute-start.3) | collective-permute-done | bytes 589856 | tf_op jit(solution)/shard_map/ppermute | solution.py:20
  86.4 9.9 %collective-permute-done.4 = bf16[256,1152]{1,0:T(8,128)(2,1)} collective-permute-done((bf16[256,1152]{1,0:T(8,128)(2,1)}, bf16[256,1152]{1,0:T(8,128)(2,1)}, u32[]{:S(2)}, u32[]{:S(2)}) %collective-permute-start.4) | collective-permute-done | bytes 589856 | tf_op jit(solution)/shard_map/ppermute | solution.py:20
  96.3 3.1 add_convert_fusion.3
  99.4 19.3 %collective-permute-done.5 = bf16[256,1152]{1,0:T(8,128)(2,1)} collective-permute-done((bf16[256,1152]{1,0:T(8,128)(2,1)}, bf16[256,1152]{1,0:T(8,128)(2,1)}, u32[]{:S(2)}, u32[]{:S(2)}) %collective-permute-start.5) | collective-permute-done | bytes 589856 | tf_op jit(solution)/shard_map/ppermute | solution.py:20
  118.7 9.0 %collective-permute-done.6 = bf16[256,1152]{1,0:T(8,128)(2,1)} collective-permute-done((bf16[256,1152]{1,0:T(8,128)(2,1)}, bf16[256,1152]{1,0:T(8,128)(2,1)}, u32[]{:S(2)}, u32[]{:S(2)}) %collective-permute-start.6) | collective-permute-done | bytes 589856 | tf_op jit(solution)/shard_map/ppermute | solution.py:20
  127.7 3.1 add_convert_fusion.2
  130.8 19.3 %collective-permute-done.7 = bf16[256,1152]{1,0:T(8,128)(2,1)} collective-permute-done((bf16[256,1152]{1,0:T(8,128)(2,1)}, bf16[256,1152]{1,0:T(8,128)(2,1)}, u32[]{:S(2)}, u32[]{:S(2)}) %collective-permute-start.7) | collective-permute-done | bytes 589856 | tf_op jit(solution)/shard_map/ppermute | solution.py:20
  150.1 8.1 %collective-permute-done.8 = bf16[256,1152]{1,0:T(8,128)(2,1)} collective-permute-done((bf16[256,1152]{1,0:T(8,128)(2,1)}, bf16[256,1152]{1,0:T(8,128)(2,1)}, u32[]{:S(2)}, u32[]{:S(2)}) %collective-permute-start.8) | collective-permute-done | bytes 589856 | tf_op jit(solution)/shard_map/ppermute | solution.py:20
  158.2 3.1 add_convert_fusion.1
  161.3 19.3 %collective-permute-done.9 = bf16[256,1152]{1,0:T(8,128)(2,1)} collective-permute-done((bf16[256,1152]{1,0:T(8,128)(2,1)}, bf16[256,1152]{1,0:T(8,128)(2,1)}, u32[]{:S(2)}, u32[]{:S(2)}) %collective-permute-start.9) | collective-permute-done | bytes 589856 | tf_op jit(solution)/shard_map/ppermute | solution.py:20
  180.6 8.7 %collective-permute-done.10 = bf16[256,1152]{1,0:T(8,128)(2,1)} collective-permute-done((bf16[256,1152]{1,0:T(8,128)(2,1)}, bf16[256,1152]{1,0:T(8,128)(2,1)}, u32[]{:S(2)}, u32[]{:S(2)}) %collective-permute-start.10) | collective-permute-done | bytes 589856 | tf_op jit(solution)/shard_map/ppermute | solution.py:20
  189.3 3.1 add_convert_fusion
  192.4 11.0 %collective-permute-done.11 = bf16[256,1152]{1,0:T(8,128)(2,1)S(1)} collective-permute-done((bf16[256,1152]{1,0:T(8,128)(2,1)}, bf16[256,1152]{1,0:T(8,128)(2,1)S(1)}, u32[]{:S(2)}, u32[]{:S(2)}) %collective-permute-start.11) | collective-permute-done | bytes 589856 | tf_op jit(solution)/shard_map/ppermute | solution.py:20
  203.4 1.6 fusion.2
  205.0 0.0 copy-start.3
  205.0 0.3 fusion.4
  205.3 0.8 copy-done.3
  206.1 2.5 fusion
  208.6 0.0 reduce-scatter.5.cloned.1.call-update
  208.6 0.0 reduce-scatter.7.cloned.1.call-start
  208.7 43.2 %reduce-scatter.5.cloned.1.call-done = bf16[1152,288]{0,1:T(8,128)(2,1)} async-done(((bf16[1152,1152]{0,1:T(8,128)(2,1)}), bf16[1152,288]{0,1:T(8,128)(2,1)}) %reduce-scatter.5.cloned.1.call-update) | async-done | bytes 663568 | tf_op jit(solution)/shard_map/reduce_scatter | solution.py:90
  251.9 2.6 copy.9
  254.5 0.0 reduce-scatter.7.cloned.1.call-update
  254.5 67.7 %reduce-scatter.7.cloned.1.call-done = f32[144,288]{1,0:T(8,128)} async-done(((f32[1152,288]{1,0:T(8,128)}), f32[144,288]{1,0:T(8,128)}) %reduce-scatter.7.cloned.1.call-update) | async-done | bytes 165904
  322.2 1.1 copy.10
  323.3 0.7 multiply_reduce_fusion.1
  323.9 1.8 fusion.1
  325.8 39.7 %psum.7 = f32[]{:T(128)} all-reduce(f32[]{:T(128)} %multiply_reduce_fusion.1), channel_id=1, replica_groups=mesh['dp'=8,'outer'=4] {'dp','outer'}, use_global_device_ids=true, to_apply=%region_6.7 | all-reduce | flops 1 | bytes 8 | tf_op jit(solution)/shard_map/psum | solution.py:94
  366.2 0.8 copy.8
  (15 shorter events, 0.1 us)
Async XLA Ops:
  7.2 1.8 copy-start
  7.2 244.7 %reduce-scatter.5.cloned.1.call-start = ((), (), s32[]{:S(2)}) async-start(), calls=%async_computation.2 | async-start | bytes 3317760 | tf_op jit(solution)/shard_map/reduce_scatter | solution.py:90
  11.1 1.0 copy-start.1
  12.2 17.7 %collective-permute-start = (bf16[256,1152]{1,0:T(8,128)(2,1)S(1)}, bf16[256,1152]{1,0:T(8,128)(2,1)}, u32[]{:S(2)}, u32[]{:S(2)}) collective-permute-start(bf16[256,1152]{1,0:T(8,128)(2,1)S(1)} %multiply_convert_fusion), channel_id=1, source_target_pairs={{0,24},{4,28},{8,0},{12,4},{16,8},{20,12},{24,16},{28,20},{1,25},{... | collective-permute-start | bytes 1769480 | tf_op jit(solution)/shard_map/ppermute | solution.py:20
  29.9 34.1 %copy-start.4 = (bf16[1,256,1152]{2,1,0:T(8,128)(2,1)S(1)}, bf16[1,256,1152]{2,1,0:T(8,128)(2,1)}, u32[]{:S(2)}) copy-start(bf16[1,256,1152]{2,1,0:T(8,128)(2,1)} %param.5) | copy-start | bytes 1769476
  33.3 19.9 %collective-permute-start.1 = (bf16[256,1152]{1,0:T(8,128)(2,1)}, bf16[256,1152]{1,0:T(8,128)(2,1)}, u32[]{:S(2)}, u32[]{:S(2)}) collective-permute-start(bf16[256,1152]{1,0:T(8,128)(2,1)} %convolution_convert_fusion.2), channel_id=1, source_target_pairs={{0,4},{4,8},{8,12},{12,16},{16,20},{20,24},{24,28},{28,0},{1,5},{5... | collective-permute-start | bytes 1769480 | tf_op jit(solution)/shard_map/ppermute | solution.py:20
  34.8 29.2 %collective-permute-start.2 = (bf16[256,1152]{1,0:T(8,128)(2,1)}, bf16[256,1152]{1,0:T(8,128)(2,1)}, u32[]{:S(2)}, u32[]{:S(2)}) collective-permute-start(bf16[256,1152]{1,0:T(8,128)(2,1)} %collective-permute-done), channel_id=1, source_target_pairs={{0,4},{4,8},{8,12},{12,16},{16,20},{20,24},{24,28},{28,0},{1,5},{5... | collective-permute-start | bytes 1769480 | tf_op jit(solution)/shard_map/ppermute | solution.py:20
  67.1 19.3 %collective-permute-start.3 = (bf16[256,1152]{1,0:T(8,128)(2,1)}, bf16[256,1152]{1,0:T(8,128)(2,1)}, u32[]{:S(2)}, u32[]{:S(2)}) collective-permute-start(bf16[256,1152]{1,0:T(8,128)(2,1)} %add_convert_fusion.4), channel_id=1, source_target_pairs={{0,4},{4,8},{8,12},{12,16},{16,20},{20,24},{24,28},{28,0},{1,5},{5... | collective-permute-start | bytes 1769480 | tf_op jit(solution)/shard_map/ppermute | solution.py:20
  67.1 29.2 %collective-permute-start.4 = (bf16[256,1152]{1,0:T(8,128)(2,1)}, bf16[256,1152]{1,0:T(8,128)(2,1)}, u32[]{:S(2)}, u32[]{:S(2)}) collective-permute-start(bf16[256,1152]{1,0:T(8,128)(2,1)} %collective-permute-done.2), channel_id=1, source_target_pairs={{0,4},{4,8},{8,12},{12,16},{16,20},{20,24},{24,28},{28,0},{1,5},{5... | collective-permute-start | bytes 1769480 | tf_op jit(solution)/shard_map/ppermute | solution.py:20
  99.4 19.3 %collective-permute-start.5 = (bf16[256,1152]{1,0:T(8,128)(2,1)}, bf16[256,1152]{1,0:T(8,128)(2,1)}, u32[]{:S(2)}, u32[]{:S(2)}) collective-permute-start(bf16[256,1152]{1,0:T(8,128)(2,1)} %add_convert_fusion.3), channel_id=1, source_target_pairs={{0,4},{4,8},{8,12},{12,16},{16,20},{20,24},{24,28},{28,0},{1,5},{5... | collective-permute-start | bytes 1769480 | tf_op jit(solution)/shard_map/ppermute | solution.py:20
  99.4 28.3 %collective-permute-start.6 = (bf16[256,1152]{1,0:T(8,128)(2,1)}, bf16[256,1152]{1,0:T(8,128)(2,1)}, u32[]{:S(2)}, u32[]{:S(2)}) collective-permute-start(bf16[256,1152]{1,0:T(8,128)(2,1)} %collective-permute-done.4), channel_id=1, source_target_pairs={{0,4},{4,8},{8,12},{12,16},{16,20},{20,24},{24,28},{28,0},{1,5},{5... | collective-permute-start | bytes 1769480 | tf_op jit(solution)/shard_map/ppermute | solution.py:20
  130.8 19.3 %collective-permute-start.7 = (bf16[256,1152]{1,0:T(8,128)(2,1)}, bf16[256,1152]{1,0:T(8,128)(2,1)}, u32[]{:S(2)}, u32[]{:S(2)}) collective-permute-start(bf16[256,1152]{1,0:T(8,128)(2,1)} %add_convert_fusion.2), channel_id=1, source_target_pairs={{0,4},{4,8},{8,12},{12,16},{16,20},{20,24},{24,28},{28,0},{1,5},{5... | collective-permute-start | bytes 1769480 | tf_op jit(solution)/shard_map/ppermute | solution.py:20
  130.8 27.4 %collective-permute-start.8 = (bf16[256,1152]{1,0:T(8,128)(2,1)}, bf16[256,1152]{1,0:T(8,128)(2,1)}, u32[]{:S(2)}, u32[]{:S(2)}) collective-permute-start(bf16[256,1152]{1,0:T(8,128)(2,1)} %collective-permute-done.6), channel_id=1, source_target_pairs={{0,4},{4,8},{8,12},{12,16},{16,20},{20,24},{24,28},{28,0},{1,5},{5... | collective-permute-start | bytes 1769480 | tf_op jit(solution)/shard_map/ppermute | solution.py:20
  161.3 19.3 %collective-permute-start.9 = (bf16[256,1152]{1,0:T(8,128)(2,1)}, bf16[256,1152]{1,0:T(8,128)(2,1)}, u32[]{:S(2)}, u32[]{:S(2)}) collective-permute-start(bf16[256,1152]{1,0:T(8,128)(2,1)} %add_convert_fusion.1), channel_id=1, source_target_pairs={{0,4},{4,8},{8,12},{12,16},{16,20},{20,24},{24,28},{28,0},{1,5},{5... | collective-permute-start | bytes 1769480 | tf_op jit(solution)/shard_map/ppermute | solution.py:20
  161.3 28.0 %collective-permute-start.10 = (bf16[256,1152]{1,0:T(8,128)(2,1)}, bf16[256,1152]{1,0:T(8,128)(2,1)}, u32[]{:S(2)}, u32[]{:S(2)}) collective-permute-start(bf16[256,1152]{1,0:T(8,128)(2,1)} %collective-permute-done.8), channel_id=1, source_target_pairs={{0,4},{4,8},{8,12},{12,16},{16,20},{20,24},{24,28},{28,0},{1,5},{5... | collective-permute-start | bytes 1769480 | tf_op jit(solution)/shard_map/ppermute | solution.py:20
  192.4 12.6 %copy-start.2 = (f32[256,1152]{1,0:T(8,128)S(1)}, f32[256,1152]{1,0:T(8,128)}, u32[]{:S(2)}) copy-start(f32[256,1152]{1,0:T(8,128)} %copy-done.1) | copy-start | bytes 3538948
  192.4 11.0 %collective-permute-start.11 = (bf16[256,1152]{1,0:T(8,128)(2,1)}, bf16[256,1152]{1,0:T(8,128)(2,1)S(1)}, u32[]{:S(2)}, u32[]{:S(2)}) collective-permute-start(bf16[256,1152]{1,0:T(8,128)(2,1)} %add_convert_fusion), channel_id=1, source_target_pairs={{0,20},{4,24},{8,28},{12,0},{16,4},{20,8},{24,12},{28,16},{1,21},{... | collective-permute-start | bytes 1769480 | tf_op jit(solution)/shard_map/ppermute | solution.py:20
  205.0 1.1 copy-start.3
  208.6 113.6 %reduce-scatter.7.cloned.1.call-start = ((), (), s32[]{:S(2)}) async-start(), calls=%async_computation.3 | async-start | bytes 1990656
Sparse Core Ops, SparseCore 0:
  208.7 43.1 reduce-scatter.4
  255.7 66.3 reduce-scatter.6
where the time goes:
time: 375 us; the launch traced here: 374 us
  waiting for transfers between devices  273 us (73%)
  blocking collectives  39.7 us (11%)
  matrix products  25.4 us (7%)
  between operations  14.8 us (4%)
  local copies, waits for them, and re-layouts  8.67 us (2%)
  starting transfers between devices  7.23 us (2%)
  other arithmetic  4.65 us (1%)
    ppermute x12, waiting for transfers between devices, shifted(): return lax.ppermute(value, axis, pairs)  162 us
    unnamed x3, waiting for transfers between devices  67.7 us
    reduce_scatter x1, waiting for transfers between devices, local(): lax.psum_scatter(partial_value.astype(jnp.bfloat16), 'outer', scatter_dim...  43.2 us
    psum x1, blocking collectives, local(): global_sq = lax.psum(jnp.sum(owned * owned), ('dp', 'outer'))  39.7 us
    dot_general x6, matrix products, local(): jnp.einsum('ik,ie->ke', weights, unit_img, preferred_element_type=jnp.flo...  18.9 us
    unnamed x13, local copies, waits for them, and re-layouts  7.99 us
  transfers between devices with their start and end apart: 14, of which 14 were waited for; matrix products, arithmetic and copies ran while one was open for 1% of the time, Pallas kernels for 0%

commit v1 on v0

--- a/solution.py
+++ b/solution.py
@@ -3,6 +3,8 @@
 import jax
 import jax.numpy as jnp
 from jax import lax
+from jax.experimental import pallas as pl
+from jax.experimental.pallas import tpu as pltpu
 from jax.sharding import PartitionSpec as P
 
 WINDOW = 6
@@ -97,6 +99,386 @@
     return (grad_text[None], owned * factor)
 
 
+CHUNKS = 2
+SLAB_LANES = 384
+Z_SIZE = 4
+QUAD = 4
+
+
+def rows_ds(start, count):
+    return pl.ds(pl.multiple_of(start, 16), count)
+
+
+def kernel(
+    image_ref, text_ref, proj_ref, step_ref, col_ref,
+    grad_text_ref, grad_proj_ref,
+    img, ftq, hs, hq, unit_text, inv_norm, units, ugrad, hgrad,
+    psend, prec, own_part, zsend, zrec, sq_src, sq_quad, sq_mid, sq_dp,
+    up_sem, down_sem, side_sem, img_recv, ft_send, ft_recv, h_send, h_recv,
+    p_send, p_recv, z_send, z_recv, q_send, q_recv, d_send, d_recv,
+):
+    bf16, f32 = jnp.bfloat16, jnp.float32
+    me = lax.axis_index("dp")
+    quad = lax.axis_index("outer")
+    n_dp = 2 * Z_SIZE
+    z, x = me // 2, me % 2
+    rows, width = image_ref.shape
+    chunk = rows // CHUNKS
+    own_rows, own_cols = grad_proj_ref.shape
+
+    def device(dp, outer):
+        return {"dp": dp, "outer": outer}
+
+    barrier = pltpu.get_barrier_semaphore()
+    for i in range(1, QUAD):
+        pl.semaphore_signal(barrier, inc=1, device_id=device(me, (quad + i) % QUAD),
+                            device_id_type=pl.DeviceIdType.MESH)
+    for i in range(1, n_dp):
+        pl.semaphore_signal(barrier, inc=1, device_id=device((me + i) % n_dp, quad),
+                            device_id_type=pl.DeviceIdType.MESH)
+
+    values = image_ref[...].astype(f32)
+    inverse = lax.rsqrt(jnp.sum(values * values, axis=-1, keepdims=True) + EPSILON)
+    img[me] = (values * inverse).astype(bf16)
+    pl.semaphore_wait(barrier, QUAD - 1 + n_dp - 1)
+
+    def image_copy(block, part, target, send_sem):
+        where = img.at[block, pl.ds(part * chunk, chunk)]
+        return pltpu.make_async_remote_copy(
+            src_ref=where, dst_ref=where, send_sem=send_sem, recv_sem=img_recv.at[block, part],
+            device_id=device(target, quad), device_id_type=pl.DeviceIdType.MESH)
+
+    def up(zs, part):
+        return image_copy(2 * zs + x, part, me + 2, up_sem.at[zs, part])
+
+    def down(zs, part):
+        return image_copy(2 * zs + x, part, me - 2, down_sem.at[zs, part])
+
+    def side(zs, part):
+        return image_copy(2 * zs + x, part, me + 1 - 2 * x, side_sem.at[zs, part])
+
+    def arrived(block, part):
+        image_copy(block, part, me, side_sem.at[0, part]).wait_recv()
+
+    def wanted(at, zs):
+        return jnp.logical_or(x == 0, (zs + 2) % Z_SIZE != at)
+
+    def reaches(at, zs):
+        inner = jnp.logical_and(at > 0, at < Z_SIZE - 1)
+        return jnp.logical_or(inner, wanted(at, zs))
+
+    def goes_side(zs):
+        ahead = (zs - z + Z_SIZE) % Z_SIZE
+        return jnp.logical_or(ahead == 1, ahead == 2 + x)
+
+    def relayed(distance, act):
+        for part in range(CHUNKS):
+            for sign in (1, -1):
+                zs = z + sign * distance
+                inside = zs < Z_SIZE if sign == 1 else zs >= 0
+                here = jnp.logical_and(inside, reaches(z, zs))
+                beyond = z - sign
+                further = beyond >= 0 if sign == 1 else beyond < Z_SIZE
+                act(zs, part, here,
+                    jnp.logical_and(jnp.logical_and(inside, further), reaches(beyond, zs)),
+                    jnp.logical_and(here, goes_side(zs)),
+                    down if sign == 1 else up)
+
+    def relay(distance):
+        def act(zs, part, here, onward, aside, onward_copy):
+            @pl.when(here)
+            def _():
+                arrived(2 * zs + x, part)
+
+                @pl.when(onward)
+                def _():
+                    onward_copy(zs, part).start()
+
+                @pl.when(aside)
+                def _():
+                    side(zs, part).start()
+
+        relayed(distance, act)
+
+    def finish_relay(distance):
+        def act(zs, part, here, onward, aside, onward_copy):
+            @pl.when(onward)
+            def _():
+                onward_copy(zs, part).wait_send()
+
+            @pl.when(aside)
+            def _():
+                side(zs, part).wait_send()
+
+        relayed(distance, act)
+
+    for part in range(CHUNKS):
+        @pl.when(z < Z_SIZE - 1)
+        def _():
+            up(z, part).start()
+
+        @pl.when(z > 0)
+        def _():
+            down(z, part).start()
+
+        side(z, part).start()
+
+    turned = text_ref[...].astype(f32).T
+    for zc in range(Z_SIZE):
+        for xc in range(2):
+            at = (2 * zc + xc) * own_rows
+            ftq[quad, pl.ds((xc * Z_SIZE + zc) * own_rows, own_rows)] = (
+                turned[at:at + own_rows].astype(bf16))
+
+    def ft_copy(source, i):
+        return pltpu.make_async_remote_copy(
+            src_ref=ftq.at[source], dst_ref=ftq.at[source], send_sem=ft_send.at[i],
+            recv_sem=ft_recv.at[source], device_id=device(me, (quad + i) % QUAD),
+            device_id_type=pl.DeviceIdType.MESH)
+
+    for i in range(1, QUAD):
+        ft_copy(quad, i).start()
+
+    hidden = jnp.dot(text_ref[...], proj_ref[...], preferred_element_type=f32)
+    inv = lax.rsqrt(jnp.sum(hidden * hidden, axis=-1, keepdims=True) + EPSILON)
+    inv_norm[...] = jnp.broadcast_to(inv, inv_norm.shape)
+    unit = hidden * inv
+    unit_text[...] = unit
+    units[...] = unit.astype(bf16)
+
+    def pair_step(block, first=False):
+        if not first:
+            for part in range(CHUNKS):
+                @pl.when(needs_wait(block))
+                def _():
+                    arrived(block, part)
+        position = (block - me + 2 + n_dp) % n_dp
+        images = img[block]
+        dots = lax.dot_general(units[...], images, (((1,), (1,)), ((), ())),
+                               preferred_element_type=f32)
+        logits = LOGIT_SCALE * dots + LOGIT_BIAS
+        columns = lax.broadcasted_iota(jnp.int32, logits.shape, 0)
+        positive = jnp.logical_and(step_ref[pl.ds(block, 1), :] == position,
+                                   col_ref[pl.ds(block, 1), :] == columns)
+        target = jnp.where(positive, 1.0, -1.0).astype(f32)
+        weights = (-LOSS_SCALE * LOGIT_SCALE * target * jax.nn.sigmoid(-target * logits)).astype(bf16)
+        term = jnp.dot(weights, images, preferred_element_type=f32)
+        if first:
+            ugrad[...] = term
+        else:
+            ugrad[...] += term
+
+    def needs_wait(block):
+        return block % 2 != x
+
+    ahead, behind = (z + 1) % Z_SIZE, (z + Z_SIZE - 1) % Z_SIZE
+    third = jnp.where(x == 0, behind, (z + 2) % Z_SIZE)
+    col_ahead, col_behind = 2 * ahead + x, 2 * behind + x
+    side_ahead, side_third = 2 * ahead + 1 - x, 2 * third + 1 - x
+    low, high = z == 0, z == Z_SIZE - 1
+    order = (
+        2 * z + 1 - x,
+        jnp.where(high, col_behind, col_ahead),
+        jnp.where(low, side_ahead, jnp.where(high, side_third, col_behind)),
+        jnp.where(low, side_third, jnp.where(high, col_ahead, side_ahead)),
+        jnp.where(low, col_behind, jnp.where(high, side_ahead, side_third)),
+    )
+    pair_step(me, first=True)
+    relay(1)
+    pair_step(order[0])
+    pair_step(order[1])
+    relay(2)
+    pair_step(order[2])
+    relay(3)
+    pair_step(order[3])
+    pair_step(order[4])
+
+    unit = unit_text[...]
+    total = ugrad[...]
+    radial = jnp.sum(unit * total, axis=-1, keepdims=True)
+    hidden_grad = (inv_norm[:, :1] * (total - unit * radial)).astype(bf16)
+    hgrad[...] = hidden_grad
+    wide = hidden_grad.astype(f32)
+    for c in range(QUAD):
+        moved = wide if c == 0 else pltpu.roll(wide, width - c * own_cols, 1)
+        hs[c] = moved[:, :SLAB_LANES].astype(bf16)
+
+    def h_copy(source, i):
+        return pltpu.make_async_remote_copy(
+            src_ref=hs.at[(quad + i) % QUAD], dst_ref=hq.at[source], send_sem=h_send.at[i],
+            recv_sem=h_recv.at[source], device_id=device(me, (quad + i) % QUAD),
+            device_id_type=pl.DeviceIdType.MESH)
+
+    for i in range(1, QUAD):
+        h_copy(quad, i).start()
+    hq[quad] = hs[quad]
+    grad_text_ref[...] = lax.dot_general(
+        hgrad[...], proj_ref[...], (((1,), (1,)), ((), ())), preferred_element_type=f32
+    ).astype(bf16)
+
+    for i in range(1, QUAD):
+        source = (quad + i) % QUAD
+        ft_copy(source, i).wait_recv()
+        h_copy(source, i).wait_recv()
+
+    half = Z_SIZE * own_rows
+
+    def half_sum(which):
+        acc = None
+        for q in range(QUAD):
+            term = jnp.dot(ftq[q, rows_ds(which * half, half)], hq[q], preferred_element_type=f32)
+            acc = term if acc is None else acc + term
+        return acc
+
+    def p_copy(zc):
+        return pltpu.make_async_remote_copy(
+            src_ref=psend.at[zc], dst_ref=prec.at[zc], send_sem=p_send.at[zc],
+            recv_sem=p_recv.at[zc], device_id=device(me + 1 - 2 * x, quad),
+            device_id_type=pl.DeviceIdType.MESH)
+
+    part_sum = half_sum(1 - x)
+    for zc in range(Z_SIZE):
+        psend[zc] = part_sum[zc * own_rows:(zc + 1) * own_rows].astype(bf16)
+        p_copy(zc).start()
+    part_sum = half_sum(x)
+    for zc in range(Z_SIZE):
+        own_part[zc] = part_sum[zc * own_rows:(zc + 1) * own_rows]
+
+    def z_copy(source, i):
+        return pltpu.make_async_remote_copy(
+            src_ref=zsend.at[i], dst_ref=zrec.at[source], send_sem=z_send.at[i],
+            recv_sem=z_recv.at[source], device_id=device((me + 2 * i) % n_dp, quad),
+            device_id_type=pl.DeviceIdType.MESH)
+
+    for i in range(1, Z_SIZE):
+        to = (z + i) % Z_SIZE
+        p_copy(to).wait_recv()
+        zsend[i] = (own_part[to] + prec[to].astype(f32)).astype(bf16)
+        z_copy(z, i).start()
+    p_copy(z).wait_recv()
+    owned = own_part[z] + prec[z].astype(f32)
+    for i in range(1, Z_SIZE):
+        source = (z + i) % Z_SIZE
+        z_copy(source, i).wait_recv()
+        owned = owned + zrec[source].astype(f32)
+
+    lanes = lax.broadcasted_iota(jnp.int32, owned.shape, 1)
+    kept = jnp.where(lanes < own_cols, owned, 0.0)
+    mine = jnp.sum(kept * kept)
+    sq_src[...] = jnp.broadcast_to(mine, sq_src.shape)
+
+    def q_copy(source, i):
+        return pltpu.make_async_remote_copy(
+            src_ref=sq_src, dst_ref=sq_quad.at[source], send_sem=q_send.at[i],
+            recv_sem=q_recv.at[source], device_id=device(me, (quad + i) % QUAD),
+            device_id_type=pl.DeviceIdType.MESH)
+
+    def d_copy(source, i):
+        return pltpu.make_async_remote_copy(
+            src_ref=sq_mid, dst_ref=sq_dp.at[source], send_sem=d_send.at[i],
+            recv_sem=d_recv.at[source], device_id=device((me + i) % n_dp, quad),
+            device_id_type=pl.DeviceIdType.MESH)
+
+    for i in range(1, QUAD):
+        q_copy(quad, i).start()
+    sq_quad[quad] = sq_src[...]
+    for i in range(1, QUAD):
+        q_copy((quad + i) % QUAD, i).wait_recv()
+    sq_mid[...] = sq_quad[0] + sq_quad[1] + sq_quad[2] + sq_quad[3]
+    for i in range(1, n_dp):
+        d_copy(me, i).start()
+    sq_dp[me] = sq_mid[...]
+
+    for part in range(CHUNKS):
+        @pl.when(z < Z_SIZE - 1)
+        def _():
+            up(z, part).wait_send()
+
+        @pl.when(z > 0)
+        def _():
+            down(z, part).wait_send()
+
+        side(z, part).wait_send()
+    for distance in range(1, Z_SIZE):
+        finish_relay(distance)
+    for i in range(1, QUAD):
+        ft_copy(quad, i).wait_send()
+        h_copy(quad, i).wait_send()
+        q_copy(quad, i).wait_send()
+    for zc in range(Z_SIZE):
+        p_copy(zc).wait_send()
+    for i in range(1, Z_SIZE):
+        z_copy(z, i).wait_send()
+
+    for i in range(1, n_dp):
+        d_copy((me + i) % n_dp, i).wait_recv()
+    global_sq = sq_dp[0]
+    for i in range(1, n_dp):
+        global_sq = global_sq + sq_dp[i]
+    threshold = math.sqrt(width * proj_ref.shape[0])
+    factor = jnp.minimum(1.0, threshold / jnp.sqrt(global_sq[:1, :1]))
+    grad_proj_ref[...] = owned[:, :own_cols] * factor
+    for i in range(1, n_dp):
+        d_copy(me, i).wait_send()
+
+
+def fused(image_embeds, text_features, projection, pair_step, pair_col):
+    n_dp, n_outer = lax.axis_size("dp"), lax.axis_size("outer")
+    rows, width = image_embeds.shape[1:]
+    depth = projection.shape[0]
+    own_rows, own_cols = depth // n_dp, width // n_outer
+    bf16, f32 = jnp.bfloat16, jnp.float32
+    dma = pltpu.SemaphoreType.DMA
+    vmem = pl.BlockSpec(memory_space=pltpu.VMEM)
+    slab = (own_rows, SLAB_LANES)
+    grad_text, grad_proj = pl.pallas_call(
+        kernel,
+        out_shape=(
+            jax.ShapeDtypeStruct((rows, depth), bf16),
+            jax.ShapeDtypeStruct((own_rows, own_cols), f32),
+        ),
+        in_specs=[vmem] * 5,
+        out_specs=(vmem, vmem),
+        scratch_shapes=[
+            pltpu.VMEM((n_dp, rows, width), bf16),
+            pltpu.VMEM((QUAD, depth, rows), bf16),
+            pltpu.VMEM((QUAD, rows, SLAB_LANES), bf16),
+            pltpu.VMEM((QUAD, rows, SLAB_LANES), bf16),
+            pltpu.VMEM((rows, width), f32),
+            pltpu.VMEM((rows, 128), f32),
+            pltpu.VMEM((rows, width), bf16),
+            pltpu.VMEM((rows, width), f32),
+            pltpu.VMEM((rows, width), bf16),
+            pltpu.VMEM((Z_SIZE, *slab), bf16),
+            pltpu.VMEM((Z_SIZE, *slab), bf16),
+            pltpu.VMEM((Z_SIZE, *slab), f32),
+            pltpu.VMEM((Z_SIZE, *slab), bf16),
+            pltpu.VMEM((Z_SIZE, *slab), bf16),
+            pltpu.VMEM((8, 128), f32),
+            pltpu.VMEM((QUAD, 8, 128), f32),
+            pltpu.VMEM((8, 128), f32),
+            pltpu.VMEM((n_dp, 8, 128), f32),
+            dma((Z_SIZE, CHUNKS)), dma((Z_SIZE, CHUNKS)), dma((Z_SIZE, CHUNKS)),
+            dma((n_dp, CHUNKS)),
+            dma((QUAD,)), dma((QUAD,)), dma((QUAD,)), dma((QUAD,)),
+            dma((Z_SIZE,)), dma((Z_SIZE,)), dma((Z_SIZE,)), dma((Z_SIZE,)),
+            dma((QUAD,)), dma((QUAD,)), dma((n_dp,)), dma((n_dp,)),
+        ],
+        compiler_params=pltpu.CompilerParams(
+            collective_id=0, has_side_effects=True, vmem_limit_bytes=48 * 1024 * 1024
+        ),
+        cost_estimate=pl.CostEstimate(
+            flops=2 * rows * depth * width * 3 + 4 * WINDOW * rows * rows * width,
+            bytes_accessed=2 * (4 * rows * width + depth * width),
+            transcendentals=WINDOW * rows * rows,
+        ),
+    )(
+        image_embeds[0], text_features[0], projection,
+        pair_step.reshape(n_dp, rows), pair_col.reshape(n_dp, rows),
+    )
+    return grad_text[None], grad_proj
+
+
 def solution(mesh):
     placed = (
         P("outer", "dp", None),
@@ -105,8 +487,9 @@
         P("outer", None),
         P("outer", None),
     )
+    small = mesh.shape["dp"] == 2 * Z_SIZE and mesh.shape["outer"] == QUAD
     return jax.shard_map(
-        local,
+        fused if small else local,
         mesh=mesh,
         in_specs=placed,
         out_specs=(P("outer", "dp", None), P("dp", "outer")),

time: 375 us -> 91.7 us (0.24)
  waiting for transfers between devices: 273 us -> 0 us
  Pallas kernels: 0 us -> 82 us
  blocking collectives: 39.7 us -> 0 us
  matrix products: 25.4 us -> 0 us
  between operations: 14.8 us -> 0.67 us
  starting transfers between devices: 7.23 us -> 0 us
    ppermute x12 -> x0, waiting for transfers between devices: 162 us -> none  [shifted(): return lax.ppermute(value, axis, pairs)]
    pallas_call x0 -> x1, Pallas kernels: none -> 82 us  [fused(): pl.pallas_call(kernel, out_shape=(jax.ShapeDtypeStruct((rows, depth), bf1...]
    unnamed x3 -> x0, waiting for transfers between devices: 67.7 us -> none
    reduce_scatter x1 -> x0, waiting for transfers between devices: 43.2 us -> none  [local(): lax.psum_scatter(partial_value.astype(jnp.bfloat16), 'outer', scatter_dim...]
    psum x1 -> x0, blocking collectives: 39.7 us -> none  [local(): global_sq = lax.psum(jnp.sum(owned * owned), ('dp', 'outer'))]
    dot_general x9 -> x0, matrix products: 25.4 us -> none  [the longest x6 18.9 us: local(): jnp.einsum('ik,ie->ke', weights, unit_img, preferred_element_type=jnp.flo...]
    ppermute x12 -> x0, starting transfers between devices: 7.15 us -> none  [shifted(): return lax.ppermute(value, axis, pairs)]
    unnamed x13 -> x9, local copies, waits for them, and re-layouts: 7.99 us -> 5.89 us
  transfers between devices with their start and end apart: 14 -> 0, of which waited for: 14 -> 0; matrix products, arithmetic and copies ran while one was open for 1% -> 0% of each run, Pallas kernels for 0% -> 0%
where the time goes in v1:
time: 91.7 us; the launch traced here: 91.3 us
  Pallas kernels  82 us (89%)
  local copies, waits for them, and re-layouts  5.9 us (6%)
  other arithmetic  2.73 us (3%)
    pallas_call x1, Pallas kernels, fused(): pl.pallas_call(kernel, out_shape=(jax.ShapeDtypeStruct((rows, depth), bf1...  82 us
    unnamed x9, local copies, waits for them, and re-layouts  5.89 us
    unnamed x2, other arithmetic  2.73 us

profile of v1, /device:TPU:0, one launch (start us, length us, event | category | flops | bytes accessed | tf_op | source)
XLA Modules:
  0.0 91.3 jit_solution(13416401776696506261)
XLA Ops:
  0.6 0.5 broadcast.6
  1.1 1.4 %reduce.6 = s32[2048]{0:T(1024)S(1)} reduce(s32[1,2048]{1,0:T(1,128)} %param.8, s32[]{:T(128)} %broadcast.6), dimensions={0}, to_apply=%param.8.reduce_sub_computation.3 | reduce | bytes 16388 | tf_op args[3]
  2.5 1.4 %reduce.7 = s32[2048]{0:T(1024)S(1)} reduce(s32[1,2048]{1,0:T(1,128)} %param.9, s32[]{:T(128)} %broadcast.6), dimensions={0}, to_apply=%param.9.reduce_sub_computation.3 | reduce | bytes 16388 | tf_op args[4]
  3.9 0.0 copy-start
  3.9 1.7 %copy-done = bf16[1152,1152]{1,0:T(8,128)(2,1)S(1)} copy-done((bf16[1152,1152]{1,0:T(8,128)(2,1)S(1)}, bf16[1152,1152]{1,0:T(8,128)(2,1)}, u32[]{:S(2)}) %copy-start) | copy-done | bytes 2654232
  5.7 0.0 copy-start.1
  5.7 1.1 %copy-done.1 = bf16[1,256,1152]{2,1,0:T(8,128)(2,1)S(1)} copy-done((bf16[1,256,1152]{2,1,0:T(8,128)(2,1)S(1)}, bf16[1,256,1152]{2,1,0:T(8,128)(2,1)}, u32[]{:S(2)}) %copy-start.1) | copy-done | bytes 589848
  6.7 0.0 copy-start.2
  6.7 1.1 %copy-done.2 = bf16[1,256,1152]{2,1,0:T(8,128)(2,1)S(1)} copy-done((bf16[1,256,1152]{2,1,0:T(8,128)(2,1)S(1)}, bf16[1,256,1152]{2,1,0:T(8,128)(2,1)}, u32[]{:S(2)}) %copy-start.2) | copy-done | bytes 589848
  7.8 82.0 %shard_map.68 = (bf16[256,1152]{1,0:T(8,128)(2,1)S(1)}, f32[144,288]{1,0:T(8,128)S(1)}) custom-call(bf16[256,1152]{1,0:T(8,128)(2,1)S(1)} %bitcast.4, bf16[256,1152]{1,0:T(8,128)(2,1)S(1)} %bitcast.5, bf16[1152,1152]{1,0:T(8,128)(2,1)S(1)} %copy-done, s32[8,256]{1,0:T(8,128)S(1)} %reshape.10.step_ref, s32[8,256]{1,0:T(8,128)S(1)} %reshape.11.col_ref), custom_call_target="tpu_custom_call" | custom-call | flops 3850371072 | bytes 5013504 | tf_op jit(solution)/shard_map/pallas_call | solution.py:434
  89.8 0.8 copy.9
  90.6 0.7 copy.10
  (2 shorter events, 0.0 us)
Async XLA Ops:
  3.9 1.8 %copy-start = (bf16[1152,1152]{1,0:T(8,128)(2,1)S(1)}, bf16[1152,1152]{1,0:T(8,128)(2,1)}, u32[]{:S(2)}) copy-start(bf16[1152,1152]{1,0:T(8,128)(2,1)} %proj_ref.1) | copy-start | bytes 7962628
  5.7 1.1 %copy-start.1 = (bf16[1,256,1152]{2,1,0:T(8,128)(2,1)S(1)}, bf16[1,256,1152]{2,1,0:T(8,128)(2,1)}, u32[]{:S(2)}) copy-start(bf16[1,256,1152]{2,1,0:T(8,128)(2,1)} %param.5) | copy-start | bytes 1769476
  6.7 1.1 %copy-start.2 = (bf16[1,256,1152]{2,1,0:T(8,128)(2,1)S(1)}, bf16[1,256,1152]{2,1,0:T(8,128)(2,1)}, u32[]{:S(2)}) copy-start(bf16[1,256,1152]{2,1,0:T(8,128)(2,1)} %param.6) | copy-start | bytes 1769476

commit v2 on v1

--- a/solution.py
+++ b/solution.py
@@ -100,7 +100,7 @@
 
 
 CHUNKS = 2
-SLAB_LANES = 384
+LANES = 128
 Z_SIZE = 4
 QUAD = 4
 
@@ -110,8 +110,9 @@
 
 
 def kernel(
-    image_ref, text_ref, proj_ref, step_ref, col_ref,
+    image_hbm, text_hbm, proj_hbm, step_hbm, col_hbm,
     grad_text_ref, grad_proj_ref,
+    image_ref, text_ref, proj_ref, step_ref, col_ref, load_sem,
     img, ftq, hs, hq, unit_text, inv_norm, units, ugrad, hgrad,
     psend, prec, own_part, zsend, zrec, sq_src, sq_quad, sq_mid, sq_dp,
     up_sem, down_sem, side_sem, img_recv, ft_send, ft_recv, h_send, h_recv,
@@ -129,6 +130,15 @@
     def device(dp, outer):
         return {"dp": dp, "outer": outer}
 
+    loads = [
+        pltpu.make_async_copy(source, target, load_sem.at[i])
+        for i, (source, target) in enumerate((
+            (image_hbm.at[0], image_ref), (text_hbm.at[0], text_ref), (proj_hbm, proj_ref),
+            (step_hbm, step_ref), (col_hbm, col_ref)))
+    ]
+    for load in loads:
+        load.start()
+
     barrier = pltpu.get_barrier_semaphore()
     for i in range(1, QUAD):
         pl.semaphore_signal(barrier, inc=1, device_id=device(me, (quad + i) % QUAD),
@@ -137,6 +147,7 @@
         pl.semaphore_signal(barrier, inc=1, device_id=device((me + i) % n_dp, quad),
                             device_id_type=pl.DeviceIdType.MESH)
 
+    loads[0].wait()
     values = image_ref[...].astype(f32)
     inverse = lax.rsqrt(jnp.sum(values * values, axis=-1, keepdims=True) + EPSILON)
     img[me] = (values * inverse).astype(bf16)
@@ -171,8 +182,8 @@
         ahead = (zs - z + Z_SIZE) % Z_SIZE
         return jnp.logical_or(ahead == 1, ahead == 2 + x)
 
-    def relayed(distance, act):
-        for part in range(CHUNKS):
+    def relayed(distance, act, parts=range(CHUNKS)):
+        for part in parts:
             for sign in (1, -1):
                 zs = z + sign * distance
                 inside = zs < Z_SIZE if sign == 1 else zs >= 0
@@ -184,7 +195,7 @@
                     jnp.logical_and(here, goes_side(zs)),
                     down if sign == 1 else up)
 
-    def relay(distance):
+    def relay(distance, parts=range(CHUNKS)):
         def act(zs, part, here, onward, aside, onward_copy):
             @pl.when(here)
             def _():
@@ -198,7 +209,7 @@
                 def _():
                     side(zs, part).start()
 
-        relayed(distance, act)
+        relayed(distance, act, parts)
 
     def finish_relay(distance):
         def act(zs, part, here, onward, aside, onward_copy):
@@ -223,6 +234,7 @@
 
         side(z, part).start()
 
+    loads[1].wait()
     turned = text_ref[...].astype(f32).T
     for zc in range(Z_SIZE):
         for xc in range(2):
@@ -239,27 +251,31 @@
     for i in range(1, QUAD):
         ft_copy(quad, i).start()
 
+    loads[2].wait()
     hidden = jnp.dot(text_ref[...], proj_ref[...], preferred_element_type=f32)
     inv = lax.rsqrt(jnp.sum(hidden * hidden, axis=-1, keepdims=True) + EPSILON)
     inv_norm[...] = jnp.broadcast_to(inv, inv_norm.shape)
     unit = hidden * inv
     unit_text[...] = unit
     units[...] = unit.astype(bf16)
-
-    def pair_step(block, first=False):
+    loads[3].wait()
+    loads[4].wait()
+
+    def pair_step(block, parts, first=False):
         if not first:
-            for part in range(CHUNKS):
+            for part in parts:
                 @pl.when(needs_wait(block))
                 def _():
                     arrived(block, part)
         position = (block - me + 2 + n_dp) % n_dp
-        images = img[block]
+        start, count = parts[0] * chunk, len(parts) * chunk
+        images = img[block, pl.ds(start, count)]
         dots = lax.dot_general(units[...], images, (((1,), (1,)), ((), ())),
                                preferred_element_type=f32)
         logits = LOGIT_SCALE * dots + LOGIT_BIAS
         columns = lax.broadcasted_iota(jnp.int32, logits.shape, 0)
-        positive = jnp.logical_and(step_ref[pl.ds(block, 1), :] == position,
-                                   col_ref[pl.ds(block, 1), :] == columns)
+        where = pl.ds(pl.multiple_of(block * rows + start, LANES), count)
+        positive = jnp.logical_and(step_ref[:, where] == position, col_ref[:, where] == columns)
         target = jnp.where(positive, 1.0, -1.0).astype(f32)
         weights = (-LOSS_SCALE * LOGIT_SCALE * target * jax.nn.sigmoid(-target * logits)).astype(bf16)
         term = jnp.dot(weights, images, preferred_element_type=f32)
@@ -283,15 +299,17 @@
         jnp.where(low, side_third, jnp.where(high, col_ahead, side_ahead)),
         jnp.where(low, col_behind, jnp.where(high, side_ahead, side_third)),
     )
-    pair_step(me, first=True)
+    every = range(CHUNKS)
+    pair_step(me, every, first=True)
     relay(1)
-    pair_step(order[0])
-    pair_step(order[1])
+    pair_step(order[0], every)
+    pair_step(order[1], every)
     relay(2)
-    pair_step(order[2])
-    relay(3)
-    pair_step(order[3])
-    pair_step(order[4])
+    pair_step(order[2], every)
+    for part in every:
+        relay(3, (part,))
+        pair_step(order[3], (part,))
+        pair_step(order[4], (part,))
 
     unit = unit_text[...]
     total = ugrad[...]
@@ -299,73 +317,89 @@
     hidden_grad = (inv_norm[:, :1] * (total - unit * radial)).astype(bf16)
     hgrad[...] = hidden_grad
     wide = hidden_grad.astype(f32)
+    slices = -(-own_cols // LANES)
     for c in range(QUAD):
         moved = wide if c == 0 else pltpu.roll(wide, width - c * own_cols, 1)
-        hs[c] = moved[:, :SLAB_LANES].astype(bf16)
-
-    def h_copy(source, i):
-        return pltpu.make_async_remote_copy(
-            src_ref=hs.at[(quad + i) % QUAD], dst_ref=hq.at[source], send_sem=h_send.at[i],
-            recv_sem=h_recv.at[source], device_id=device(me, (quad + i) % QUAD),
-            device_id_type=pl.DeviceIdType.MESH)
-
-    for i in range(1, QUAD):
-        h_copy(quad, i).start()
+        for s in range(slices):
+            hs[c, s] = moved[:, s * LANES:(s + 1) * LANES].astype(bf16)
+
+    def h_copy(source, i, s):
+        return pltpu.make_async_remote_copy(
+            src_ref=hs.at[(quad + i) % QUAD, s], dst_ref=hq.at[source, s],
+            send_sem=h_send.at[i, s], recv_sem=h_recv.at[source, s],
+            device_id=device(me, (quad + i) % QUAD), device_id_type=pl.DeviceIdType.MESH)
+
+    for s in range(slices):
+        for i in range(1, QUAD):
+            h_copy(quad, i, s).start()
     hq[quad] = hs[quad]
-    grad_text_ref[...] = lax.dot_general(
+    grad_text_ref[0] = lax.dot_general(
         hgrad[...], proj_ref[...], (((1,), (1,)), ((), ())), preferred_element_type=f32
     ).astype(bf16)
 
     for i in range(1, QUAD):
-        source = (quad + i) % QUAD
-        ft_copy(source, i).wait_recv()
-        h_copy(source, i).wait_recv()
+        ft_copy((quad + i) % QUAD, i).wait_recv()
 
     half = Z_SIZE * own_rows
 
-    def half_sum(which):
+    def half_sum(which, s):
         acc = None
         for q in range(QUAD):
-            term = jnp.dot(ftq[q, rows_ds(which * half, half)], hq[q], preferred_element_type=f32)
+            term = jnp.dot(ftq[q, rows_ds(which * half, half)], hq[q, s],
+                           preferred_element_type=f32)
             acc = term if acc is None else acc + term
         return acc
 
-    def p_copy(zc):
-        return pltpu.make_async_remote_copy(
-            src_ref=psend.at[zc], dst_ref=prec.at[zc], send_sem=p_send.at[zc],
-            recv_sem=p_recv.at[zc], device_id=device(me + 1 - 2 * x, quad),
+    def p_copy(zc, s):
+        return pltpu.make_async_remote_copy(
+            src_ref=psend.at[s, zc], dst_ref=prec.at[s, zc], send_sem=p_send.at[zc, s],
+            recv_sem=p_recv.at[zc, s], device_id=device(me + 1 - 2 * x, quad),
             device_id_type=pl.DeviceIdType.MESH)
 
-    part_sum = half_sum(1 - x)
-    for zc in range(Z_SIZE):
-        psend[zc] = part_sum[zc * own_rows:(zc + 1) * own_rows].astype(bf16)
-        p_copy(zc).start()
-    part_sum = half_sum(x)
-    for zc in range(Z_SIZE):
-        own_part[zc] = part_sum[zc * own_rows:(zc + 1) * own_rows]
-
-    def z_copy(source, i):
-        return pltpu.make_async_remote_copy(
-            src_ref=zsend.at[i], dst_ref=zrec.at[source], send_sem=z_send.at[i],
-            recv_sem=z_recv.at[source], device_id=device((me + 2 * i) % n_dp, quad),
+    def z_copy(source, i, s):
+        return pltpu.make_async_remote_copy(
+            src_ref=zsend.at[s, i], dst_ref=zrec.at[s, source], send_sem=z_send.at[i, s],
+            recv_sem=z_recv.at[source, s], device_id=device((me + 2 * i) % n_dp, quad),
             device_id_type=pl.DeviceIdType.MESH)
 
-    for i in range(1, Z_SIZE):
-        to = (z + i) % Z_SIZE
-        p_copy(to).wait_recv()
-        zsend[i] = (own_part[to] + prec[to].astype(f32)).astype(bf16)
-        z_copy(z, i).start()
-    p_copy(z).wait_recv()
-    owned = own_part[z] + prec[z].astype(f32)
-    for i in range(1, Z_SIZE):
-        source = (z + i) % Z_SIZE
-        z_copy(source, i).wait_recv()
-        owned = owned + zrec[source].astype(f32)
-
-    lanes = lax.broadcasted_iota(jnp.int32, owned.shape, 1)
-    kept = jnp.where(lanes < own_cols, owned, 0.0)
-    mine = jnp.sum(kept * kept)
-    sq_src[...] = jnp.broadcast_to(mine, sq_src.shape)
+    def send_half(s):
+        for i in range(1, QUAD):
+            h_copy((quad + i) % QUAD, i, s).wait_recv()
+        part_sum = half_sum(1 - x, s)
+        for zc in range(Z_SIZE):
+            psend[s, zc] = part_sum[zc * own_rows:(zc + 1) * own_rows].astype(bf16)
+            p_copy(zc, s).start()
+        part_sum = half_sum(x, s)
+        for zc in range(Z_SIZE):
+            own_part[s, zc] = part_sum[zc * own_rows:(zc + 1) * own_rows]
+
+    def send_owners(s):
+        for i in (2, 1, 3):
+            to = (z + i) % Z_SIZE
+            p_copy(to, s).wait_recv()
+            zsend[s, i] = (own_part[s, to] + prec[s, to].astype(f32)).astype(bf16)
+            z_copy(z, i, s).start()
+
+    def finished(s):
+        p_copy(z, s).wait_recv()
+        owned = own_part[s, z] + prec[s, z].astype(f32)
+        for i in range(1, Z_SIZE):
+            source = (z + i) % Z_SIZE
+            z_copy(source, i, s).wait_recv()
+            owned = owned + zrec[s, source].astype(f32)
+        lanes = lax.broadcasted_iota(jnp.int32, owned.shape, 1)
+        return jnp.where(lanes < own_cols - s * LANES, owned, 0.0)
+
+    for s in range(slices):
+        send_half(s)
+        if s > 0:
+            send_owners(s - 1)
+    send_owners(slices - 1)
+    owned = [finished(s) for s in range(slices)]
+    squares = owned[0] * owned[0]
+    for piece in owned[1:]:
+        squares = squares + piece * piece
+    sq_src[...] = jnp.broadcast_to(jnp.sum(squares), sq_src.shape)
 
     def q_copy(source, i):
         return pltpu.make_async_remote_copy(
@@ -403,12 +437,14 @@
         finish_relay(distance)
     for i in range(1, QUAD):
         ft_copy(quad, i).wait_send()
-        h_copy(quad, i).wait_send()
+        for s in range(slices):
+            h_copy(quad, i, s).wait_send()
         q_copy(quad, i).wait_send()
-    for zc in range(Z_SIZE):
-        p_copy(zc).wait_send()
-    for i in range(1, Z_SIZE):
-        z_copy(z, i).wait_send()
+    for s in range(slices):
+        for zc in range(Z_SIZE):
+            p_copy(zc, s).wait_send()
+        for i in range(1, Z_SIZE):
+            z_copy(z, i, s).wait_send()
 
     for i in range(1, n_dp):
         d_copy((me + i) % n_dp, i).wait_recv()
@@ -417,7 +453,9 @@
         global_sq = global_sq + sq_dp[i]
     threshold = math.sqrt(width * proj_ref.shape[0])
     factor = jnp.minimum(1.0, threshold / jnp.sqrt(global_sq[:1, :1]))
-    grad_proj_ref[...] = owned[:, :own_cols] * factor
+    for s in range(slices):
+        count = min(LANES, own_cols - s * LANES)
+        grad_proj_ref[:, s * LANES:s * LANES + count] = owned[s][:, :count] * factor
     for i in range(1, n_dp):
         d_copy(me, i).wait_send()
 
@@ -430,42 +468,51 @@
     bf16, f32 = jnp.bfloat16, jnp.float32
     dma = pltpu.SemaphoreType.DMA
     vmem = pl.BlockSpec(memory_space=pltpu.VMEM)
-    slab = (own_rows, SLAB_LANES)
+    anywhere = pl.BlockSpec(memory_space=pl.ANY)
+    slices = -(-own_cols // LANES)
+    slab = (own_rows, LANES)
     grad_text, grad_proj = pl.pallas_call(
         kernel,
         out_shape=(
-            jax.ShapeDtypeStruct((rows, depth), bf16),
+            jax.ShapeDtypeStruct((1, rows, depth), bf16),
             jax.ShapeDtypeStruct((own_rows, own_cols), f32),
         ),
-        in_specs=[vmem] * 5,
+        in_specs=[anywhere] * 5,
         out_specs=(vmem, vmem),
         scratch_shapes=[
+            pltpu.VMEM((rows, width), bf16),
+            pltpu.VMEM((rows, depth), bf16),
+            pltpu.VMEM((depth, width), bf16),
+            pltpu.VMEM((1, n_dp * rows), jnp.int32),
+            pltpu.VMEM((1, n_dp * rows), jnp.int32),
+            dma((5,)),
             pltpu.VMEM((n_dp, rows, width), bf16),
             pltpu.VMEM((QUAD, depth, rows), bf16),
-            pltpu.VMEM((QUAD, rows, SLAB_LANES), bf16),
-            pltpu.VMEM((QUAD, rows, SLAB_LANES), bf16),
+            pltpu.VMEM((QUAD, slices, rows, LANES), bf16),
+            pltpu.VMEM((QUAD, slices, rows, LANES), bf16),
             pltpu.VMEM((rows, width), f32),
             pltpu.VMEM((rows, 128), f32),
             pltpu.VMEM((rows, width), bf16),
             pltpu.VMEM((rows, width), f32),
             pltpu.VMEM((rows, width), bf16),
-            pltpu.VMEM((Z_SIZE, *slab), bf16),
-            pltpu.VMEM((Z_SIZE, *slab), bf16),
-            pltpu.VMEM((Z_SIZE, *slab), f32),
-            pltpu.VMEM((Z_SIZE, *slab), bf16),
-            pltpu.VMEM((Z_SIZE, *slab), bf16),
+            pltpu.VMEM((slices, Z_SIZE, *slab), bf16),
+            pltpu.VMEM((slices, Z_SIZE, *slab), bf16),
+            pltpu.VMEM((slices, Z_SIZE, *slab), f32),
+            pltpu.VMEM((slices, Z_SIZE, *slab), bf16),
+            pltpu.VMEM((slices, Z_SIZE, *slab), bf16),
             pltpu.VMEM((8, 128), f32),
             pltpu.VMEM((QUAD, 8, 128), f32),
             pltpu.VMEM((8, 128), f32),
             pltpu.VMEM((n_dp, 8, 128), f32),
             dma((Z_SIZE, CHUNKS)), dma((Z_SIZE, CHUNKS)), dma((Z_SIZE, CHUNKS)),
             dma((n_dp, CHUNKS)),
-            dma((QUAD,)), dma((QUAD,)), dma((QUAD,)), dma((QUAD,)),
-            dma((Z_SIZE,)), dma((Z_SIZE,)), dma((Z_SIZE,)), dma((Z_SIZE,)),
+            dma((QUAD,)), dma((QUAD,)), dma((QUAD, slices)), dma((QUAD, slices)),
+            dma((Z_SIZE, slices)), dma((Z_SIZE, slices)),
+            dma((Z_SIZE, slices)), dma((Z_SIZE, slices)),
             dma((QUAD,)), dma((QUAD,)), dma((n_dp,)), dma((n_dp,)),
         ],
         compiler_params=pltpu.CompilerParams(
-            collective_id=0, has_side_effects=True, vmem_limit_bytes=48 * 1024 * 1024
+            collective_id=0, has_side_effects=True, vmem_limit_bytes=60 * 1024 * 1024
         ),
         cost_estimate=pl.CostEstimate(
             flops=2 * rows * depth * width * 3 + 4 * WINDOW * rows * rows * width,
@@ -473,10 +520,9 @@
             transcendentals=WINDOW * rows * rows,
         ),
     )(
-        image_embeds[0], text_features[0], projection,
-        pair_step.reshape(n_dp, rows), pair_col.reshape(n_dp, rows),
-    )
-    return grad_text[None], grad_proj
+        image_embeds, text_features, projection, pair_step, pair_col
+    )
+    return grad_text, grad_proj
 
 
 def solution(mesh):

time: 91.7 us -> 85.6 us (0.933)
  other arithmetic: 2.73 us -> 0 us
  local copies, waits for them, and re-layouts: 5.9 us -> 3.56 us
    unnamed x2 -> x0, other arithmetic: 2.73 us -> none
    unnamed x9 -> x2, local copies, waits for them, and re-layouts: 5.89 us -> 3.56 us
where the time goes in v2:
time: 85.6 us; the launch traced here: 85.4 us
  Pallas kernels  81.2 us (95%)
  local copies, waits for them, and re-layouts  3.56 us (4%)
    pallas_call x1, Pallas kernels, fused(): pl.pallas_call(kernel, out_shape=(jax.ShapeDtypeStruct((1, rows, depth),...  81.2 us
    unnamed x2, local copies, waits for them, and re-layouts  3.56 us

profile of v2, /device:TPU:0, one launch (start us, length us, event | category | flops | bytes accessed | tf_op | source)
XLA Modules:
  0.0 85.4 jit_solution(10450346404057229400)
XLA Ops:
  0.6 81.2 %shard_map.68 = (bf16[1,256,1152]{2,1,0:T(8,128)(2,1)}, f32[144,288]{1,0:T(8,128)}) custom-call(bf16[1,256,1152]{2,1,0:T(8,128)(2,1)} %image_hbm.1, bf16[1,256,1152]{2,1,0:T(8,128)(2,1)} %text_hbm.1, bf16[1152,1152]{1,0:T(8,128)(2,1)} %proj_hbm.1, s32[1,2048]{1,0:T(1,128)} %step_hbm.1, s32[1,2048]{1,0:T(1,128)} %col_hbm.1), custom_call_target="tpu_custom_call" | custom-call | flops 3850371072 | bytes 5013504 | tf_op jit(solution)/shard_map/pallas_call | solution.py:474
  81.9 1.9 %copy.9 = bf16[1,256,1152]{2,1,0:T(8,128)(2,1)} copy(bf16[1,256,1152]{2,1,0:T(8,128)(2,1)} %get-tuple-element.4) | data formatting | bytes 1179648
  83.8 1.6 %copy.10 = f32[144,288]{1,0:T(8,128)} copy(f32[144,288]{1,0:T(8,128)} %get-tuple-element.5) | data formatting | bytes 331776

commit v3 on v2

--- a/solution.py
+++ b/solution.py
@@ -99,7 +99,7 @@
     return (grad_text[None], owned * factor)
 
 
-CHUNKS = 2
+CHUNKS = 4
 LANES = 128
 Z_SIZE = 4
 QUAD = 4
@@ -115,7 +115,7 @@
     image_ref, text_ref, proj_ref, step_ref, col_ref, load_sem,
     img, ftq, hs, hq, unit_text, inv_norm, units, ugrad, hgrad,
     psend, prec, own_part, zsend, zrec, sq_src, sq_quad, sq_mid, sq_dp,
-    up_sem, down_sem, side_sem, img_recv, ft_send, ft_recv, h_send, h_recv,
+    up_sem, down_sem, side_sem, side_two_sem, pass_sem, img_recv, ft_send, ft_recv, h_send, h_recv,
     p_send, p_recv, z_send, z_recv, q_send, q_recv, d_send, d_recv,
 ):
     bf16, f32 = jnp.bfloat16, jnp.float32
@@ -159,80 +159,33 @@
             src_ref=where, dst_ref=where, send_sem=send_sem, recv_sem=img_recv.at[block, part],
             device_id=device(target, quad), device_id_type=pl.DeviceIdType.MESH)
 
-    def up(zs, part):
-        return image_copy(2 * zs + x, part, me + 2, up_sem.at[zs, part])
-
-    def down(zs, part):
-        return image_copy(2 * zs + x, part, me - 2, down_sem.at[zs, part])
-
-    def side(zs, part):
-        return image_copy(2 * zs + x, part, me + 1 - 2 * x, side_sem.at[zs, part])
+    ahead, behind = (z + 1) % Z_SIZE, (z + Z_SIZE - 1) % Z_SIZE
+    partner = me + 1 - 2 * x
+    col_ahead, col_behind = 2 * ahead + x, 2 * behind + x
+    side_ahead = 2 * ahead + 1 - x
+    third = jnp.where(x == 0, 2 * behind + 1, 2 * ((z + 2) % Z_SIZE))
+    passed = jnp.where(x == 0, me + 1, 2 * ahead)
+    passed_to = jnp.where(x == 0, col_ahead, col_behind)
+
+    def own_copies(part):
+        return (
+            image_copy(me, part, col_ahead, up_sem.at[part]),
+            image_copy(me, part, col_behind, down_sem.at[part]),
+            image_copy(me, part, partner, side_sem.at[part]),
+        )
+
+    def side_copy(part):
+        return image_copy(col_ahead, part, partner, side_two_sem.at[part])
+
+    def passed_copy(part):
+        return image_copy(passed, part, passed_to, pass_sem.at[part])
 
     def arrived(block, part):
-        image_copy(block, part, me, side_sem.at[0, part]).wait_recv()
-
-    def wanted(at, zs):
-        return jnp.logical_or(x == 0, (zs + 2) % Z_SIZE != at)
-
-    def reaches(at, zs):
-        inner = jnp.logical_and(at > 0, at < Z_SIZE - 1)
-        return jnp.logical_or(inner, wanted(at, zs))
-
-    def goes_side(zs):
-        ahead = (zs - z + Z_SIZE) % Z_SIZE
-        return jnp.logical_or(ahead == 1, ahead == 2 + x)
-
-    def relayed(distance, act, parts=range(CHUNKS)):
-        for part in parts:
-            for sign in (1, -1):
-                zs = z + sign * distance
-                inside = zs < Z_SIZE if sign == 1 else zs >= 0
-                here = jnp.logical_and(inside, reaches(z, zs))
-                beyond = z - sign
-                further = beyond >= 0 if sign == 1 else beyond < Z_SIZE
-                act(zs, part, here,
-                    jnp.logical_and(jnp.logical_and(inside, further), reaches(beyond, zs)),
-                    jnp.logical_and(here, goes_side(zs)),
-                    down if sign == 1 else up)
-
-    def relay(distance, parts=range(CHUNKS)):
-        def act(zs, part, here, onward, aside, onward_copy):
-            @pl.when(here)
-            def _():
-                arrived(2 * zs + x, part)
-
-                @pl.when(onward)
-                def _():
-                    onward_copy(zs, part).start()
-
-                @pl.when(aside)
-                def _():
-                    side(zs, part).start()
-
-        relayed(distance, act, parts)
-
-    def finish_relay(distance):
-        def act(zs, part, here, onward, aside, onward_copy):
-            @pl.when(onward)
-            def _():
-                onward_copy(zs, part).wait_send()
-
-            @pl.when(aside)
-            def _():
-                side(zs, part).wait_send()
-
-        relayed(distance, act)
+        image_copy(block, part, partner, side_sem.at[part]).wait_recv()
 
     for part in range(CHUNKS):
-        @pl.when(z < Z_SIZE - 1)
-        def _():
-            up(z, part).start()
-
-        @pl.when(z > 0)
-        def _():
-            down(z, part).start()
-
-        side(z, part).start()
+        for copy in own_copies(part):
+            copy.start()
 
     loads[1].wait()
     turned = text_ref[...].astype(f32).T
@@ -262,11 +215,6 @@
     loads[4].wait()
 
     def pair_step(block, parts, first=False):
-        if not first:
-            for part in parts:
-                @pl.when(needs_wait(block))
-                def _():
-                    arrived(block, part)
         position = (block - me + 2 + n_dp) % n_dp
         start, count = parts[0] * chunk, len(parts) * chunk
         images = img[block, pl.ds(start, count)]
@@ -284,32 +232,36 @@
         else:
             ugrad[...] += term
 
-    def needs_wait(block):
-        return block % 2 != x
-
-    ahead, behind = (z + 1) % Z_SIZE, (z + Z_SIZE - 1) % Z_SIZE
-    third = jnp.where(x == 0, behind, (z + 2) % Z_SIZE)
-    col_ahead, col_behind = 2 * ahead + x, 2 * behind + x
-    side_ahead, side_third = 2 * ahead + 1 - x, 2 * third + 1 - x
-    low, high = z == 0, z == Z_SIZE - 1
-    order = (
-        2 * z + 1 - x,
-        jnp.where(high, col_behind, col_ahead),
-        jnp.where(low, side_ahead, jnp.where(high, side_third, col_behind)),
-        jnp.where(low, side_third, jnp.where(high, col_ahead, side_ahead)),
-        jnp.where(low, col_behind, jnp.where(high, side_ahead, side_third)),
-    )
     every = range(CHUNKS)
+    halves = (every[:CHUNKS // 2], every[CHUNKS // 2:])
     pair_step(me, every, first=True)
-    relay(1)
-    pair_step(order[0], every)
-    pair_step(order[1], every)
-    relay(2)
-    pair_step(order[2], every)
     for part in every:
-        relay(3, (part,))
-        pair_step(order[3], (part,))
-        pair_step(order[4], (part,))
+        arrived(col_ahead, part)
+        side_copy(part).start()
+        arrived(partner, part)
+
+        @pl.when(x == 0)
+        def _():
+            passed_copy(part).start()
+
+    pair_step(partner, every)
+    pair_step(col_ahead, every)
+    for part in every:
+        arrived(col_behind, part)
+    pair_step(col_behind, every)
+    for parts in halves:
+        for part in parts:
+            arrived(side_ahead, part)
+
+            @pl.when(x == 1)
+            def _():
+                passed_copy(part).start()
+
+        pair_step(side_ahead, parts)
+    for parts in halves:
+        for part in parts:
+            arrived(third, part)
+        pair_step(third, parts)
 
     unit = unit_text[...]
     total = ugrad[...]
@@ -353,7 +305,7 @@
     def p_copy(zc, s):
         return pltpu.make_async_remote_copy(
             src_ref=psend.at[s, zc], dst_ref=prec.at[s, zc], send_sem=p_send.at[zc, s],
-            recv_sem=p_recv.at[zc, s], device_id=device(me + 1 - 2 * x, quad),
+            recv_sem=p_recv.at[zc, s], device_id=device(partner, quad),
             device_id_type=pl.DeviceIdType.MESH)
 
     def z_copy(source, i, s):
@@ -424,17 +376,8 @@
     sq_dp[me] = sq_mid[...]
 
     for part in range(CHUNKS):
-        @pl.when(z < Z_SIZE - 1)
-        def _():
-            up(z, part).wait_send()
-
-        @pl.when(z > 0)
-        def _():
-            down(z, part).wait_send()
-
-        side(z, part).wait_send()
-    for distance in range(1, Z_SIZE):
-        finish_relay(distance)
+        for copy in (*own_copies(part), side_copy(part), passed_copy(part)):
+            copy.wait_send()
     for i in range(1, QUAD):
         ft_copy(quad, i).wait_send()
         for s in range(slices):
@@ -504,7 +447,7 @@
             pltpu.VMEM((QUAD, 8, 128), f32),
             pltpu.VMEM((8, 128), f32),
             pltpu.VMEM((n_dp, 8, 128), f32),
-            dma((Z_SIZE, CHUNKS)), dma((Z_SIZE, CHUNKS)), dma((Z_SIZE, CHUNKS)),
+            dma((CHUNKS,)), dma((CHUNKS,)), dma((CHUNKS,)), dma((CHUNKS,)), dma((CHUNKS,)),
             dma((n_dp, CHUNKS)),
             dma((QUAD,)), dma((QUAD,)), dma((QUAD, slices)), dma((QUAD, slices)),
             dma((Z_SIZE, slices)), dma((Z_SIZE, slices)),
@@ -522,7 +465,27 @@
     )(
         image_embeds, text_features, projection, pair_step, pair_col
     )
-    return grad_text, grad_proj
+    return pl.pallas_call(
+        copy_out,
+        out_shape=(
+            jax.ShapeDtypeStruct(grad_text.shape, bf16), jax.ShapeDtypeStruct(grad_proj.shape, f32)
+        ),
+        in_specs=[anywhere] * 2,
+        out_specs=(anywhere, anywhere),
+        scratch_shapes=[dma((2,))],
+        compiler_params=pltpu.CompilerParams(vmem_limit_bytes=60 * 1024 * 1024),
+    )(grad_text, grad_proj)
+
+
+def copy_out(text_from, proj_from, text_to, proj_to, sems):
+    copies = (
+        pltpu.make_async_copy(text_from, text_to, sems.at[0]),
+        pltpu.make_async_copy(proj_from, proj_to, sems.at[1]),
+    )
+    for copy in copies:
+        copy.start()
+    for copy in copies:
+        copy.wait()
 
 
 def solution(mesh):

time: 85.6 us -> 106 us (1.24)
  Pallas kernels: 81.2 us -> 106 us
  local copies, waits for them, and re-layouts: 3.56 us -> 0 us
    pallas_call x0 -> x1, Pallas kernels: none -> 25.7 us  [fused(): pl.pallas_call(copy_out, out_shape=(jax.ShapeDtypeStruct(grad_text.shape,...]
    unnamed x2 -> x0, local copies, waits for them, and re-layouts: 3.56 us -> none
    pallas_call x1, Pallas kernels: 81.2 us -> 79.9 us  [fused(): pl.pallas_call(kernel, out_shape=(jax.ShapeDtypeStruct((1, rows, depth),...]
where the time goes in v3:
time: 106 us
  Pallas kernels  106 us (100%)
    pallas_call x1, Pallas kernels, fused(): pl.pallas_call(kernel, out_shape=(jax.ShapeDtypeStruct((1, rows, depth),...  79.9 us
    pallas_call x1, Pallas kernels, fused(): pl.pallas_call(copy_out, out_shape=(jax.ShapeDtypeStruct(grad_text.shape,...  25.7 us

profile of v3, /device:TPU:0, one launch (start us, length us, event | category | flops | bytes accessed | tf_op | source)
XLA Modules:
  0.0 106.2 jit_solution(17264799768585315372)
XLA Ops:
  0.6 79.9 %shard_map.68 = (bf16[1,256,1152]{2,1,0:T(8,128)(2,1)}, f32[144,288]{1,0:T(8,128)}) custom-call(bf16[1,256,1152]{2,1,0:T(8,128)(2,1)} %image_hbm.1, bf16[1,256,1152]{2,1,0:T(8,128)(2,1)} %text_hbm.1, bf16[1152,1152]{1,0:T(8,128)(2,1)} %proj_hbm.1, s32[1,2048]{1,0:T(1,128)} %step_hbm.1, s32[1,2048]{1,0:T(1,128)} %col_hbm.1), custom_call_target="tpu_custom_call" | custom-call | flops 3850371072 | bytes 5013504 | tf_op jit(solution)/shard_map/pallas_call | solution.py:417
  80.5 25.7 %shard_map.69 = (bf16[1,256,1152]{2,1,0:T(8,128)(2,1)}, f32[144,288]{1,0:T(8,128)}) custom-call(bf16[1,256,1152]{2,1,0:T(8,128)(2,1)} %get-tuple-element.4.text_from, f32[144,288]{1,0:T(8,128)} %get-tuple-element.5.proj_from), custom_call_target="tpu_custom_call" | custom-call | tf_op jit(solution)/shard_map/pallas_call | solution.py:468

commit v4 on v3

--- a/solution.py
+++ b/solution.py
@@ -470,22 +470,14 @@
         out_shape=(
             jax.ShapeDtypeStruct(grad_text.shape, bf16), jax.ShapeDtypeStruct(grad_proj.shape, f32)
         ),
-        in_specs=[anywhere] * 2,
-        out_specs=(anywhere, anywhere),
-        scratch_shapes=[dma((2,))],
-        compiler_params=pltpu.CompilerParams(vmem_limit_bytes=60 * 1024 * 1024),
+        in_specs=[vmem] * 2,
+        out_specs=(vmem, vmem),
     )(grad_text, grad_proj)
 
 
-def copy_out(text_from, proj_from, text_to, proj_to, sems):
-    copies = (
-        pltpu.make_async_copy(text_from, text_to, sems.at[0]),
-        pltpu.make_async_copy(proj_from, proj_to, sems.at[1]),
-    )
-    for copy in copies:
-        copy.start()
-    for copy in copies:
-        copy.wait()
+def copy_out(text_from, proj_from, text_to, proj_to):
+    text_to[...] = text_from[...]
+    proj_to[...] = proj_from[...]
 
 
 def solution(mesh):

time: 106 us -> 82.7 us (0.78)
  Pallas kernels: 106 us -> 81.9 us
    pallas_call x1, Pallas kernels: 25.7 us -> 2.04 us  [fused(): pl.pallas_call(copy_out, out_shape=(jax.ShapeDtypeStruct(grad_text.shape,...]
where the time goes in v4:
time: 82.7 us; the launch traced here: 82.5 us
  Pallas kernels  81.9 us (99%)
    pallas_call x1, Pallas kernels, fused(): pl.pallas_call(kernel, out_shape=(jax.ShapeDtypeStruct((1, rows, depth),...  79.9 us
    pallas_call x1, Pallas kernels, fused(): pl.pallas_call(copy_out, out_shape=(jax.ShapeDtypeStruct(grad_text.shape,...  2.04 us

profile of v4, /device:TPU:0, one launch (start us, length us, event | category | flops | bytes accessed | tf_op | source)
XLA Modules:
  0.0 82.5 jit_solution(972051515447774017)
XLA Ops:
  0.6 79.9 %shard_map.68 = (bf16[1,256,1152]{2,1,0:T(8,128)(2,1)}, f32[144,288]{1,0:T(8,128)}) custom-call(bf16[1,256,1152]{2,1,0:T(8,128)(2,1)} %image_hbm.1, bf16[1,256,1152]{2,1,0:T(8,128)(2,1)} %text_hbm.1, bf16[1152,1152]{1,0:T(8,128)(2,1)} %proj_hbm.1, s32[1,2048]{1,0:T(1,128)} %step_hbm.1, s32[1,2048]{1,0:T(1,128)} %col_hbm.1), custom_call_target="tpu_custom_call" | custom-call | flops 3850371072 | bytes 5013504 | tf_op jit(solution)/shard_map/pallas_call | solution.py:417
  80.5 2.0 %shard_map.69 = (bf16[1,256,1152]{2,1,0:T(8,128)(2,1)}, f32[144,288]{1,0:T(8,128)}) custom-call(bf16[1,256,1152]{2,1,0:T(8,128)(2,1)} %get-tuple-element.4.text_from, f32[144,288]{1,0:T(8,128)} %get-tuple-element.5.proj_from), custom_call_target="tpu_custom_call" | custom-call | tf_op jit(solution)/shard_map/pallas_call | solution.py:468
